TPU v7x, 512 devices: a whole 4x8x8 slice. The times are simulated.
512 devices in a mesh: dp: 16 (over z_lo, x), ctx: 32 (over y, z_hi, core).
Axes of the slice: x: 4, y: 8, z: 8 (z_hi: 2, z_lo: 4; z = z_hi * 4 + z_lo), core: 2. Of those that a mesh axis runs over, the one named last changes fastest.
Arguments:
- queries: bfloat16 [16, 4096, 512], P('dp', 'ctx'), may hold values from -6 to 6
- key_states: bfloat16 [16, 4096, 512], P('dp', 'ctx'), may hold values from -6 to 6
- value_states: bfloat16 [16, 4096, 512], P('dp', 'ctx'), may hold values from -6 to 6
- gate_states: bfloat16 [16, 4096, 512], P('dp', 'ctx'), may hold values from -6 to 6
- out_grad: bfloat16 [16, 4096, 512], P('dp', 'ctx'), may hold values from -6 to 6
- segment_ids: int32 [16, 4096], P('dp'), may hold values from 0 to 3, never falling along the last dimension, each value on 1 to 2048 neighbouring positions
- norm_gain: float32 [512], replicated, may hold values from 0.1 to 1.9
Outputs:
- layer_out: bfloat16 [16, 4096, 512], P('dp', 'ctx')
- query_grad: bfloat16 [16, 4096, 512], P('dp', 'ctx')
- key_grad: bfloat16 [16, 4096, 512], P('dp', 'ctx')
- value_grad: bfloat16 [16, 4096, 512], P('dp', 'ctx')
- gate_grad: bfloat16 [16, 4096, 512], P('dp', 'ctx')
- gain_grad: float32 [512], replicated
Inputs may be any that keep to these rules, and one draw needn't show every extreme that they name: `segment_ids`: in each sample the history numbers never fall, each of the 4 histories has 1 to 2048 positions and one has exactly 2048.
All inputs are finite; a program needn't handle non-finite values.
Results may differ from a plain program's by a relative error of at most 0.0058.
Values may be sent and summed in bfloat16 or wider, within the bound.
No kernel may reach another device: no remote copies, remote signals or barrier semaphores. Data moves between devices by JAX's collectives and lax.ppermute only.
A program may use at most 64 MiB of HBM per device.

v0:
```python
import math
import jax
import jax.numpy as jnp
from jax import lax
from jax.sharding import PartitionSpec as P

HEADS = 4
HSIZE = 128


def head_dot(left_rows, right_rows):
    left_heads = left_rows.reshape(left_rows.shape[0], HEADS, HSIZE)
    right_heads = right_rows.reshape(right_rows.shape[0], HEADS, HSIZE)
    return jnp.einsum("qhd,khd->hqk", left_heads, right_heads, preferred_element_type=jnp.float32)


def head_product(weights, rows):
    rows_heads = rows.reshape(rows.shape[0], HEADS, HSIZE)
    result = jnp.einsum("hqk,khd->qhd", weights, rows_heads, preferred_element_type=jnp.float32)
    return result.reshape(result.shape[0], HEADS * HSIZE)


def head_product_back(weights, rows):
    rows_heads = rows.reshape(rows.shape[0], HEADS, HSIZE)
    result = jnp.einsum("hqk,qhd->khd", weights, rows_heads, preferred_element_type=jnp.float32)
    return result.reshape(result.shape[0], HEADS * HSIZE)


def visible_pairs(query_seg, key_seg):
    return (query_seg[:, None] == key_seg[None, :])[None]


def silu_slope(scores):
    sigmoid = jax.nn.sigmoid(scores)
    return sigmoid * (1.0 + scores * (1.0 - sigmoid))


def per_device(queries, key_states, value_states, gate_states, out_grad, segment_ids, norm_gain):
    scale = HSIZE ** (-0.5)
    tok_rows = queries.shape[1]
    hidden = queries.shape[2]
    seq_len = segment_ids.shape[1]
    segs = segment_ids[0]
    my_first = lax.axis_index("ctx") * tok_rows
    own_seg = lax.dynamic_slice_in_dim(segs, my_first, tok_rows, 0)
    own_query = queries[0]
    own_key = key_states[0]
    own_value = value_states[0]
    all_keys, all_values = (
        lax.all_gather(key_states, "ctx", axis=1, tiled=True),
        lax.all_gather(value_states, "ctx", axis=1, tiled=True),
    )
    all_keys = all_keys[0]
    all_values = all_values[0]
    block = math.gcd(seq_len, 512)
    blocks_count = seq_len // block

    def forward_step(block_id, running):
        key_first = block_id * block
        key_block = lax.dynamic_slice_in_dim(all_keys, key_first, block, 0)
        value_block = lax.dynamic_slice_in_dim(all_values, key_first, block, 0)
        key_seg = lax.dynamic_slice_in_dim(segs, key_first, block, 0)
        scores = scale * head_dot(own_query, key_block)
        visible = visible_pairs(own_seg, key_seg)
        weights = jnp.where(visible, jax.nn.silu(scores), 0.0).astype(jnp.bfloat16)
        return running + head_product(weights, value_block)

    attended = lax.fori_loop(
        0, blocks_count, forward_step, jnp.zeros((tok_rows, hidden), jnp.float32)
    )
    inv_rms = lax.rsqrt(jnp.mean(attended * attended, axis=1, keepdims=True) + 1e-06)
    normed = attended * inv_rms
    gain_row = norm_gain[None, :]
    gate_f = gate_states[0].astype(jnp.float32)
    grad_f = out_grad[0].astype(jnp.float32)
    layer_out = (normed * gain_row * gate_f).astype(jnp.bfloat16)
    gate_grad = (grad_f * normed * gain_row).astype(jnp.bfloat16)
    gain_part = jnp.sum(grad_f * normed * gate_f, axis=0)
    total_rows = lax.axis_size("dp") * lax.axis_size("ctx") * tok_rows
    gain_grad = lax.psum(gain_part, ("dp", "ctx")) / math.sqrt(total_rows)
    normed_grad = grad_f * gain_row * gate_f
    attn_grad = (
        inv_rms * (normed_grad - normed * jnp.mean(normed * normed_grad, axis=1, keepdims=True))
    ).astype(jnp.bfloat16)

    def query_step(block_id, running):
        key_first = block_id * block
        key_block = lax.dynamic_slice_in_dim(all_keys, key_first, block, 0)
        value_block = lax.dynamic_slice_in_dim(all_values, key_first, block, 0)
        key_seg = lax.dynamic_slice_in_dim(segs, key_first, block, 0)
        scores = scale * head_dot(own_query, key_block)
        visible = visible_pairs(own_seg, key_seg)
        value_dot = head_dot(attn_grad, value_block)
        slopes = jnp.where(visible, scale * value_dot * silu_slope(scores), 0.0).astype(
            jnp.bfloat16
        )
        return running + head_product(slopes, key_block)

    query_grad = lax.fori_loop(
        0, blocks_count, query_step, jnp.zeros((tok_rows, hidden), jnp.float32)
    )
    zeros_block = jnp.zeros((tok_rows, hidden), jnp.float32)
    grad_piece = attn_grad[None]
    query_rows = lax.all_gather(queries, "ctx", axis=1, tiled=True)[0]
    grad_rows = lax.all_gather(grad_piece, "ctx", axis=1, tiled=True)[0]
    row_count = grad_rows.shape[0]
    step_rows = math.gcd(row_count, 512)

    def key_step(block_id, totals):
        row_first = block_id * step_rows
        query_block = lax.dynamic_slice_in_dim(query_rows, row_first, step_rows, 0)
        grad_block = lax.dynamic_slice_in_dim(grad_rows, row_first, step_rows, 0)
        query_seg = lax.dynamic_slice_in_dim(segs, row_first, step_rows, 0)
        scores = scale * head_dot(query_block, own_key)
        visible = visible_pairs(query_seg, own_seg)
        weights = jnp.where(visible, jax.nn.silu(scores), 0.0).astype(jnp.bfloat16)
        value_dot = head_dot(grad_block, own_value)
        slopes = jnp.where(visible, scale * value_dot * silu_slope(scores), 0.0).astype(
            jnp.bfloat16
        )
        return (
            totals[0] + head_product_back(slopes, query_block),
            totals[1] + head_product_back(weights, grad_block),
        )

    key_grad, value_grad = lax.fori_loop(
        0, row_count // step_rows, key_step, (zeros_block, zeros_block)
    )
    return (
        layer_out[None],
        query_grad.astype(jnp.bfloat16)[None],
        key_grad.astype(jnp.bfloat16)[None],
        value_grad.astype(jnp.bfloat16)[None],
        gate_grad[None],
        gain_grad,
    )


def solution(mesh):
    return jax.shard_map(
        per_device,
        mesh=mesh,
        in_specs=(
            P("dp", "ctx", None),
            P("dp", "ctx", None),
            P("dp", "ctx", None),
            P("dp", "ctx", None),
            P("dp", "ctx", None),
            P("dp", None),
            P(),
        ),
        out_specs=(
            P("dp", "ctx", None),
            P("dp", "ctx", None),
            P("dp", "ctx", None),
            P("dp", "ctx", None),
            P("dp", "ctx", None),
            P(),
        ),
        check_vma=False,
    )
```

profile of v0, /device:TPU:1, one launch (start us, length us, event | category | flops | bytes accessed | tf_op | source)
XLA Modules:
  0.0 511.9 jit_solution(14382006248976778904)
XLA Ops:
  7.2 1.7 copy.34
  9.7 1.7 copy.38
  13.4 1.6 reshape_squeeze.36
  15.6 111.8 %all-gather.8.cloned.1.call-done = bf16[1,4096,512]{1,2,0:T(8,128)(2,1)} async-done(((bf16[1,128,512]{1,2,0:T(8,128)(2,1)}), bf16[1,4096,512]{1,2,0:T(8,128)(2,1)}) %all-gather.8.cloned.1.call-update) | async-done | bytes 4194320 | tf_op jit(solution)/shard_map/all_gather | solution.py:50
  127.4 104.0 %all-gather.6.cloned.1.call-done = bf16[1,4096,512]{2,1,0:T(8,128)(2,1)} async-done(((bf16[1,128,512]{2,1,0:T(8,128)(2,1)}), bf16[1,4096,512]{2,1,0:T(8,128)(2,1)}) %all-gather.6.cloned.1.call-update) | async-done | bytes 4194320 | tf_op jit(solution)/shard_map/all_gather | solution.py:51
  231.4 32.6 %while.47 = (s32[]{:T(128)}, f32[128,512]{0,1:T(8,128)S(1)}, bf16[4096,512]{1,0:T(8,128)(2,1)}, s32[128]{0:T(128)S(1)}, s32[4096]{0:T(1024)}, /*index=5*/bf16[40...) while((s32[]{:T(128)}, f32[128,512]{0,1:T(8,128)S(1)}, ...), condition=%wide.wide.region_1.2_spmd.clone, body=%wide.wide.region_0.1_spmd.clone.sunk | while | flops 136249344 | bytes 5511865 | solution.py:68
  232.4 1.1 constant_dynamic-slice_fusion.15
  233.7 1.1 constant_dynamic-slice_fusion.16
  236.4 1.1 constant_dynamic-slice_fusion.15
  237.7 1.1 constant_dynamic-slice_fusion.16
  240.5 1.1 constant_dynamic-slice_fusion.15
  241.8 1.1 constant_dynamic-slice_fusion.16
  244.6 1.1 constant_dynamic-slice_fusion.15
  245.9 1.1 constant_dynamic-slice_fusion.16
  248.6 1.1 constant_dynamic-slice_fusion.15
  249.9 1.1 constant_dynamic-slice_fusion.16
  252.7 1.1 constant_dynamic-slice_fusion.15
  254.0 1.1 constant_dynamic-slice_fusion.16
  256.8 1.1 constant_dynamic-slice_fusion.15
  258.1 1.1 constant_dynamic-slice_fusion.16
  260.8 1.1 constant_dynamic-slice_fusion.15
  262.1 1.1 constant_dynamic-slice_fusion.16
  265.9 41.7 %while.48 = (s32[]{:T(128)}, f32[128,512]{0,1:T(8,128)S(1)}, bf16[4096,512]{0,1:T(8,128)(2,1)}, s32[128]{0:T(128)S(1)}, s32[4096]{0:T(1024)}, /*index=5*/bf16[40...) while((s32[]{:T(128)}, f32[128,512]{0,1:T(8,128)S(1)}, ...), condition=%wide.wide.region_5.6_spmd.clone, body=%wide.wide.region_4.5_spmd.clone.sunk | while | flops 204668928 | bytes 6429377 | solution.py:99
  266.0 1.1 constant_dynamic-slice_fusion.17
  269.4 1.7 fusion.118
  271.2 1.1 constant_dynamic-slice_fusion.17
  274.6 1.7 fusion.118
  276.4 1.1 constant_dynamic-slice_fusion.17
  279.8 1.7 fusion.118
  281.6 1.2 constant_dynamic-slice_fusion.17
  285.1 1.7 fusion.118
  286.9 1.1 constant_dynamic-slice_fusion.17
  290.3 1.7 fusion.118
  292.1 1.1 constant_dynamic-slice_fusion.17
  295.5 1.7 fusion.118
  297.3 1.1 constant_dynamic-slice_fusion.17
  300.7 1.7 fusion.118
  302.5 1.1 constant_dynamic-slice_fusion.17
  305.9 1.7 fusion.118
  308.5 101.4 %psum.7 = f32[512]{0:T(512)S(1)} all-reduce(f32[512]{0:T(512)S(1)} %get-tuple-element.541), channel_id=1, replica_groups=mesh['dp'=16,'ctx'=32] {'dp','ctx'}, use_global_device_ids=true, to_apply=%region_9.10 | all-reduce | flops 512 | bytes 4096 | tf_op jit(solution)/shard_map/psum | solution.py:80
  410.4 32.7 %all-gather.12.cloned.1.call-done = bf16[4096,512]{1,0:T(8,128)(2,1)} async-done(((bf16[128,512]{1,0:T(8,128)(2,1)}), bf16[4096,512]{1,0:T(8,128)(2,1)}) %all-gather.12.cloned.1.call-update) | async-done | bytes 4194320 | tf_op jit(solution)/shard_map/all_gather | solution.py:105
  443.1 60.7 %while.49 = (s32[]{:T(128)}, f32[128,512]{0,1:T(8,128)S(1)}, f32[128,512]{0,1:T(8,128)S(1)}, bf16[4096,512]{0,1:T(8,128)(2,1)}, s32[4096]{0:T(1024)}, /*index=5*...) while((s32[]{:T(128)}, f32[128,512]{0,1:T(8,128)S(1)}, ...), condition=%wide.wide.region_7.8_spmd.clone, body=%wide.wide.region_6.7_spmd.clone.sunk | while | flops 273481728 | bytes 11475685 | solution.py:126
  444.2 1.3 convolution_multiply_fusion.7
  448.5 1.6 fusion.126
  450.7 1.1 constant_dynamic-slice_fusion.19
  451.8 1.3 convolution_multiply_fusion.7
  456.0 1.6 fusion.126
  458.3 1.1 constant_dynamic-slice_fusion.19
  459.4 1.3 convolution_multiply_fusion.7
  463.6 1.6 fusion.126
  465.9 1.1 constant_dynamic-slice_fusion.19
  467.0 1.3 convolution_multiply_fusion.7
  471.2 1.6 fusion.126
  473.5 1.1 constant_dynamic-slice_fusion.19
  474.6 1.3 convolution_multiply_fusion.7
  478.8 1.6 fusion.126
  481.1 1.1 constant_dynamic-slice_fusion.19
  482.2 1.3 convolution_multiply_fusion.7
  486.4 1.6 fusion.126
  488.7 1.1 constant_dynamic-slice_fusion.19
  489.8 1.3 convolution_multiply_fusion.7
  494.0 1.6 fusion.126
  497.3 1.3 convolution_multiply_fusion.7
  501.6 1.6 fusion.126
  (188 shorter events, 72.3 us)
Async XLA Ops:
  7.2 120.3 %all-gather.8.cloned.1.call-start = ((), (), s32[]{:S(2)}) async-start(), calls=%async_computation.1 | async-start | bytes 4325376 | tf_op jit(solution)/shard_map/all_gather | solution.py:50
  8.9 222.5 %all-gather.6.cloned.1.call-start = ((), (), s32[]{:S(2)}) async-start(), calls=%async_computation | async-start | bytes 4325376 | tf_op jit(solution)/shard_map/all_gather | solution.py:51
  9.7 400.7 %all-gather.10.cloned.1.call-start = ((), (), s32[]{:S(2)}) async-start(), calls=%async_computation.2 | async-start | bytes 4325376 | tf_op jit(solution)/shard_map/all_gather | solution.py:104
  11.4 431.7 %all-gather.12.cloned.1.call-start = ((), (), s32[]{:S(2)}) async-start(), calls=%async_computation.3 | async-start | bytes 4325376 | tf_op jit(solution)/shard_map/all_gather | solution.py:105
  231.4 32.8 %copy-start.2 = (bf16[1,128,512]{2,1,0:T(8,128)(2,1)S(1)}, bf16[1,128,512]{2,1,0:T(8,128)(2,1)}, u32[]{:S(2)}) copy-start(bf16[1,128,512]{2,1,0:T(8,128)(2,1)} %param.17) | copy-start | bytes 393220
  231.4 32.8 %copy-start.3 = (bf16[1,128,512]{2,1,0:T(8,128)(2,1)S(1)}, bf16[1,128,512]{2,1,0:T(8,128)(2,1)}, u32[]{:S(2)}) copy-start(bf16[1,128,512]{2,1,0:T(8,128)(2,1)} %param.16) | copy-start | bytes 393220
  231.4 32.8 %copy-start.4 = (f32[512]{0:T(512)S(1)}, f32[512]{0:T(512)}, u32[]{:S(2)}) copy-start(f32[512]{0:T(512)} %param.19) | copy-start | bytes 6148
  265.9 177.2 %copy-start = (bf16[1,128,512]{2,1,0:T(8,128)(2,1)S(1)}, bf16[1,128,512]{2,1,0:T(8,128)(2,1)}, u32[]{:S(2)}) copy-start(bf16[1,128,512]{2,1,0:T(8,128)(2,1)} %param.15) | copy-start | bytes 393220
  448.3 1.7 copy-start.1
  455.9 1.7 copy-start.1
  463.5 1.7 copy-start.1
  471.1 1.7 copy-start.1
  478.7 1.7 copy-start.1
  486.3 1.7 copy-start.1
  493.8 1.7 copy-start.1
  501.4 1.7 copy-start.1
Sparse Core Ops, SparseCore 0:
  11.7 115.6 all-gather.7
  130.8 100.6 all-gather.5
  235.1 103.4 all-gather.9
  342.4 100.7 all-gather.11
where the time goes:
time: 516 us; the launch traced here: 512 us
  waiting for transfers between devices  249 us (48%)
  blocking collectives  101 us (20%)
  local copies, waits for them, and re-layouts  84.2 us (16%)
  matrix products  48.8 us (9%)
  between operations  13.9 us (3%)
  other arithmetic  12.6 us (2%)
    all_gather x1, waiting for transfers between devices, per_device(): lax.all_gather(key_states, 'ctx', axis=1, tiled=True)  112 us
    all_gather x1, waiting for transfers between devices, per_device(): lax.all_gather(value_states, 'ctx', axis=1, tiled=True)  104 us
    psum x1, blocking collectives, per_device(): gain_grad = lax.psum(gain_part, ('dp', 'ctx')) / math.sqrt(total_rows)  101 us
    all_gather x1, waiting for transfers between devices, per_device(): grad_rows = lax.all_gather(grad_piece, 'ctx', axis=1, tiled=True)[0]  32.7 us
    dot_general x16, matrix products, head_product(): jnp.einsum('hqk,khd->qhd', weights, rows_heads, preferred_element_type=jn...  19.3 us
    dot_general x16, matrix products, head_product_back(): jnp.einsum('hqk,qhd->khd', weights, rows_heads, preferred_element_type=jn...  16.7 us
    dot_general x16, matrix products, head_dot(): jnp.einsum('qhd,khd->hqk', left_heads, right_heads, preferred_element_typ...  12.8 us
    dynamic_slice x16, local copies, waits for them, and re-layouts, forward_step(): value_block = lax.dynamic_slice_in_dim(all_values, key_first, block, 0)  10.4 us
  transfers between devices with their start and end apart: 4, of which 3 were waited for; matrix products, arithmetic and copies ran while one was open for 16% of the time, Pallas kernels for 0%

commit v1 on v0

--- a/solution.py
+++ b/solution.py
@@ -77,7 +77,7 @@
     gate_grad = (grad_f * normed * gain_row).astype(jnp.bfloat16)
     gain_part = jnp.sum(grad_f * normed * gate_f, axis=0)
     total_rows = lax.axis_size("dp") * lax.axis_size("ctx") * tok_rows
-    gain_grad = lax.psum(gain_part, ("dp", "ctx")) / math.sqrt(total_rows)
+    gain_grad = jnp.sum(lax.all_gather(gain_part, ("dp", "ctx")), axis=0) / math.sqrt(total_rows)
     normed_grad = grad_f * gain_row * gate_f
     attn_grad = (
         inv_rms * (normed_grad - normed * jnp.mean(normed * normed_grad, axis=1, keepdims=True))

time: 516 us -> 1260 us (2.44)
  waiting for transfers between devices: 249 us -> 1130 us
  blocking collectives: 101 us -> 0 us
  local copies, waits for them, and re-layouts: 84.2 us -> 68.9 us
  matrix products: 48.8 us -> 34.3 us
    all_gather x0 -> x1, waiting for transfers between devices: none -> 699 us  [per_device(): lax.all_gather(gain_part, ('dp', 'ctx'))]
    all_gather x1, waiting for transfers between devices: 0.01 us -> 106 us  [per_device(): query_rows = lax.all_gather(queries, 'ctx', axis=1, tiled=True)[0]]
    psum x1 -> x0, blocking collectives: 101 us -> none  [per_device(): gain_grad = lax.psum(gain_part, ('dp', 'ctx')) / math.sqrt(total_rows)]
    all_gather x1, waiting for transfers between devices: 32.7 us -> 104 us  [per_device(): grad_rows = lax.all_gather(grad_piece, 'ctx', axis=1, tiled=True)[0]]
  transfers between devices with their start and end apart: 4 -> 5, of which waited for: 3 -> 5; matrix products, arithmetic and copies ran while one was open for 16% -> 4% of each run, Pallas kernels for 0% -> 0%
where the time goes in v1:
time: 1260 us
  waiting for transfers between devices  1130 us (90%)
  local copies, waits for them, and re-layouts  68.9 us (5%)
  matrix products  34.3 us (3%)
  between operations  13.9 us (1%)
    all_gather x1, waiting for transfers between devices, per_device(): lax.all_gather(gain_part, ('dp', 'ctx'))  699 us
    all_gather x1, waiting for transfers between devices, per_device(): lax.all_gather(value_states, 'ctx', axis=1, tiled=True)  115 us
    all_gather x1, waiting for transfers between devices, per_device(): lax.all_gather(key_states, 'ctx', axis=1, tiled=True)  107 us
    all_gather x1, waiting for transfers between devices, per_device(): query_rows = lax.all_gather(queries, 'ctx', axis=1, tiled=True)[0]  106 us
    all_gather x1, waiting for transfers between devices, per_device(): grad_rows = lax.all_gather(grad_piece, 'ctx', axis=1, tiled=True)[0]  104 us
  transfers between devices with their start and end apart: 5, of which 5 were waited for; matrix products, arithmetic and copies ran while one was open for 4% of the time, Pallas kernels for 0%

profile of v1, /device:TPU:1, one launch (start us, length us, event | category | flops | bytes accessed | tf_op | source)
XLA Modules:
  0.0 1260.0 jit_solution(10519574359270290174)
XLA Ops:
  7.2 1.7 copy.72
  9.0 1.7 copy.73
  10.7 0.9 reshape_squeeze.32
  12.3 115.1 %all-gather.9.cloned.1.call-done = bf16[1,4096,512]{1,2,0:T(8,128)(2,1)} async-done(((bf16[1,128,512]{1,2,0:T(8,128)(2,1)}), bf16[1,4096,512]{1,2,0:T(8,128)(2,1)}) %all-gather.9.cloned.1.call-update) | async-done | bytes 4194320 | tf_op jit(solution)/shard_map/all_gather | solution.py:51
  127.4 106.9 %all-gather.11.cloned.1.call-done = bf16[1,4096,512]{1,2,0:T(8,128)(2,1)} async-done(((bf16[1,128,512]{1,2,0:T(8,128)(2,1)}), bf16[1,4096,512]{1,2,0:T(8,128)(2,1)}) %all-gather.11.cloned.1.call-update) | async-done | bytes 4194320 | tf_op jit(solution)/shard_map/all_gather | solution.py:50
  234.3 23.7 %while.47 = (s32[]{:T(128)}, f32[128,512]{0,1:T(8,128)S(1)}, bf16[4096,512]{0,1:T(8,128)(2,1)}, s32[128]{0:T(128)S(1)}, s32[4096]{0:T(1024)}, /*index=5*/bf16[40...) while((s32[]{:T(128)}, f32[128,512]{0,1:T(8,128)S(1)}, ...), condition=%wide.wide.region_1.2_spmd.clone, body=%wide.wide.region_0.1_spmd.clone.sunk | while | flops 136249344 | bytes 4463285 | solution.py:68
  234.4 1.3 constant_dynamic-slice_fusion.14
  235.7 0.8 dynamic_slice.101
  237.4 1.3 constant_dynamic-slice_fusion.14
  238.7 0.8 dynamic_slice.101
  240.3 1.3 constant_dynamic-slice_fusion.14
  241.6 0.8 dynamic_slice.101
  243.3 1.3 constant_dynamic-slice_fusion.14
  244.6 0.8 dynamic_slice.101
  246.3 1.3 constant_dynamic-slice_fusion.14
  247.5 0.8 dynamic_slice.101
  249.2 1.3 constant_dynamic-slice_fusion.14
  250.5 0.8 dynamic_slice.101
  252.2 1.3 constant_dynamic-slice_fusion.14
  253.5 0.8 dynamic_slice.101
  255.1 1.3 constant_dynamic-slice_fusion.14
  256.4 0.8 dynamic_slice.101
  258.3 1.5 fusion.59
  259.9 1.7 copy.76
  261.6 0.9 reshape_squeeze.34
  263.3 0.8 multiply_convert_fusion.1
  264.1 34.4 %while.48 = (s32[]{:T(128)}, f32[128,512]{0,1:T(8,128)S(1)}, bf16[4096,512]{0,1:T(8,128)(2,1)}, s32[128]{0:T(128)S(1)}, s32[4096]{0:T(1024)}, /*index=5*/bf16[40...) while((s32[]{:T(128)}, f32[128,512]{0,1:T(8,128)S(1)}, ...), condition=%wide.wide.region_5.6_spmd.clone, body=%wide.wide.region_4.5_spmd.clone.sunk | while | flops 204668928 | bytes 7215805 | solution.py:99
  264.2 1.3 constant_dynamic-slice_fusion.15
  266.7 1.7 fusion.123
  268.5 1.3 constant_dynamic-slice_fusion.15
  271.0 1.7 fusion.123
  272.8 1.3 constant_dynamic-slice_fusion.15
  275.3 1.7 fusion.123
  277.1 1.3 constant_dynamic-slice_fusion.15
  279.6 1.7 fusion.123
  281.4 1.3 constant_dynamic-slice_fusion.15
  283.9 1.7 fusion.123
  285.7 1.3 constant_dynamic-slice_fusion.15
  288.2 1.7 fusion.123
  290.0 1.3 constant_dynamic-slice_fusion.15
  292.5 1.7 fusion.123
  294.3 1.3 constant_dynamic-slice_fusion.15
  296.8 1.7 fusion.123
  299.3 698.6 %all-gather.17.cloned.1.call-done = f32[512,1,512]{2,1,0:T(1,128)} async-done(((f32[1,1,512]{2,1,0:T(1,128)}), f32[512,1,512]{2,1,0:T(1,128)}) %all-gather.17.cloned.1.call-update) | async-done | bytes 1048592 | tf_op jit(solution)/shard_map/all_gather | solution.py:80
  997.9 1.8 reduce_sum.39
  1000.3 106.2 %all-gather.13.cloned.1.call-done = bf16[1,4096,512]{1,2,0:T(8,128)(2,1)} async-done(((bf16[1,128,512]{1,2,0:T(8,128)(2,1)}), bf16[1,4096,512]{1,2,0:T(8,128)(2,1)}) %all-gather.13.cloned.1.call-update) | async-done | bytes 4194320 | tf_op jit(solution)/shard_map/all_gather | solution.py:104
  1106.5 104.4 %all-gather.15.cloned.1.call-done = bf16[4096,512]{1,0:T(8,128)(2,1)} async-done(((bf16[128,512]{1,0:T(8,128)(2,1)}), bf16[4096,512]{1,0:T(8,128)(2,1)}) %all-gather.15.cloned.1.call-update) | async-done | bytes 4194320 | tf_op jit(solution)/shard_map/all_gather | solution.py:105
  1210.9 41.0 %while.49 = (s32[]{:T(128)}, f32[128,512]{0,1:T(8,128)S(1)}, f32[128,512]{0,1:T(8,128)S(1)}, bf16[4096,512]{0,1:T(8,128)(2,1)}, s32[4096]{0:T(1024)}, /*index=5*...) while((s32[]{:T(128)}, f32[128,512]{0,1:T(8,128)S(1)}, ...), condition=%wide.wide.region_7.8_spmd.clone, body=%wide.wide.region_6.7_spmd.clone.sunk | while | flops 273481728 | bytes 11475693 | solution.py:126
  1210.9 1.1 constant_dynamic-slice_fusion.17
  1213.3 1.1 constant_dynamic-slice_fusion.16
  1216.0 1.1 constant_dynamic-slice_fusion.17
  1218.4 1.1 constant_dynamic-slice_fusion.16
  1221.2 1.1 constant_dynamic-slice_fusion.17
  1223.5 1.1 constant_dynamic-slice_fusion.16
  1226.3 1.1 constant_dynamic-slice_fusion.17
  1228.7 1.1 constant_dynamic-slice_fusion.16
  1231.4 1.1 constant_dynamic-slice_fusion.17
  1233.8 1.1 constant_dynamic-slice_fusion.16
  1236.5 1.1 constant_dynamic-slice_fusion.17
  1238.9 1.1 constant_dynamic-slice_fusion.16
  1241.7 1.1 constant_dynamic-slice_fusion.17
  1244.1 1.1 constant_dynamic-slice_fusion.16
  1246.8 1.1 constant_dynamic-slice_fusion.17
  1249.2 1.1 constant_dynamic-slice_fusion.16
  (163 shorter events, 44.9 us)
Async XLA Ops:
  7.2 120.3 %all-gather.9.cloned.1.call-start = ((), (), s32[]{:S(2)}) async-start(), calls=%async_computation | async-start | bytes 4325376 | tf_op jit(solution)/shard_map/all_gather | solution.py:51
  8.9 225.4 %all-gather.11.cloned.1.call-start = ((), (), s32[]{:S(2)}) async-start(), calls=%async_computation.1 | async-start | bytes 4325376 | tf_op jit(solution)/shard_map/all_gather | solution.py:50
  10.6 987.2 %all-gather.17.cloned.1.call-start = ((), (), s32[]{:S(2)}) async-start(), calls=%async_computation.4 | async-start | bytes 1050624 | tf_op jit(solution)/shard_map/all_gather | solution.py:80
  234.3 24.0 %copy-start = (bf16[1,128,512]{2,1,0:T(8,128)(2,1)S(1)}, bf16[1,128,512]{2,1,0:T(8,128)(2,1)}, u32[]{:S(2)}) copy-start(bf16[1,128,512]{2,1,0:T(8,128)(2,1)} %param.17) | copy-start | bytes 393220
  234.3 24.0 %copy-start.1 = (bf16[1,128,512]{2,1,0:T(8,128)(2,1)S(1)}, bf16[1,128,512]{2,1,0:T(8,128)(2,1)}, u32[]{:S(2)}) copy-start(bf16[1,128,512]{2,1,0:T(8,128)(2,1)} %param.16) | copy-start | bytes 393220
  234.3 24.0 %copy-start.5 = (f32[512]{0:T(512)S(1)}, f32[512]{0:T(512)}, u32[]{:S(2)}) copy-start(f32[512]{0:T(512)} %param.19) | copy-start | bytes 6148
  234.3 28.3 %copy-start.3 = (bf16[1,128,512]{2,1,0:T(8,128)(2,1)S(1)}, bf16[1,128,512]{2,1,0:T(8,128)(2,1)}, u32[]{:S(2)}) copy-start(bf16[1,128,512]{2,1,0:T(8,128)(2,1)} %param.14) | copy-start | bytes 393220
  234.3 28.3 %copy-start.2 = (bf16[1,128,512]{2,1,0:T(8,128)(2,1)S(1)}, bf16[1,128,512]{2,1,0:T(8,128)(2,1)}, u32[]{:S(2)}) copy-start(bf16[1,128,512]{2,1,0:T(8,128)(2,1)} %param.15) | copy-start | bytes 393220
  259.8 846.7 %all-gather.13.cloned.1.call-start = ((), (), s32[]{:S(2)}) async-start(), calls=%async_computation.2 | async-start | bytes 4325376 | tf_op jit(solution)/shard_map/all_gather | solution.py:104
  261.6 949.3 %all-gather.15.cloned.1.call-start = ((), (), s32[]{:S(2)}) async-start(), calls=%async_computation.3 | async-start | bytes 4325376 | tf_op jit(solution)/shard_map/all_gather | solution.py:105
  1210.9 3.7 copy-start.4
  1216.0 3.7 copy-start.4
  1221.1 3.7 copy-start.4
  1226.3 3.7 copy-start.4
  1231.4 3.7 copy-start.4
  1236.5 3.7 copy-start.4
  1241.7 3.7 copy-start.4
  1246.8 3.7 copy-start.4
Sparse Core Ops, SparseCore 0:
  11.7 115.6 all-gather.8
  131.1 103.1 all-gather.10
  259.9 737.9 all-gather.16
  1001.5 104.9 all-gather.12
  1110.2 100.6 all-gather.14
